TPU v7x, 512 devices: a whole 4x8x8 slice. The times are simulated.
512 devices in a mesh: row: 16 (over z, core), col: 32 (over x, y).
Axes of the slice: x: 4, y: 8, z: 8, core: 2. Of those that a mesh axis runs over, the one named last changes fastest.
Arguments:
- front: float32 [12288, 12288], P('row', 'col'), as said below
- structure: int32 [3, 96], replicated, may hold values from 0 to 1, as said below
- factor_front: float32 [3, 12288, 512], P(None, 'row', 'col'), may hold values from -0.0546875 to 0.0546875
- factor_border: float32 [2, 512, 512], replicated, may hold values from -0.6 to 0.6
- pivot_inverse: float32 [3, 512, 512], P(None, 'row')
Outputs:
- inverse_front: float32 [3, 512, 12288], P(None, 'row', 'col')
- inverse_parent: float32 [2, 512, 512], P(None, 'row')
- inverse_diagonal: float32 [3, 512, 512], P(None, 'row')
Inputs may be any that keep to these rules, and one draw needn't show every extreme that they name: front is exactly symmetric. structure[k, b] = 1 where front block b (rows b * 128 to (b + 1) * 128 - 1) lies in supernode k's structure; every 1 in row k is also a 1 in row k - 1; blocks b < 24 are 1 in every row.
All inputs are finite; a program needn't handle non-finite values.
Results may differ from a plain program's by a relative error of at most 0.0001.
Values sent between devices are 32-bit elements; how exact they have to be, the bound alone decides.
A program may use at most 64 MiB of HBM per device.

v0:
```python
import jax
import jax.numpy as jnp
from jax import lax
from jax.sharding import Mesh
from jax.sharding import PartitionSpec as P

BLK = 128
ROW = ("row_0", "row_1")


HIGH = lax.Precision.HIGHEST


def broadcast_by_axis(x, axes, root):
    x = jnp.where(lax.axis_index(axes) == root, x, jnp.zeros_like(x))
    for axis in axes:
        x = lax.psum(x, axis)
    return x


def split_up(x, dim, length):
    dims = x.shape
    pieces = x.reshape(*dims[:dim], length, dims[dim] // length, *dims[dim + 1 :])
    return jnp.moveaxis(pieces, dim, 0)


def sent_and_summed(x, axis, dim):
    length = lax.axis_size(axis)
    pieces = lax.all_to_all(split_up(x, dim, length), axis, 0, 0, tiled=True)
    return jnp.sum(pieces, axis=0)


def padded_to(lines, length):
    spare = -lines.shape[0] % length
    if not spare:
        return lines
    return jnp.concatenate([lines, jnp.zeros((spare, *lines.shape[1:]), lines.dtype)])


def in_order(pieces, dim):
    pieces = jnp.moveaxis(pieces, 0, dim)
    dims = pieces.shape
    return pieces.reshape(*dims[:dim], dims[dim] * dims[dim + 1], *dims[dim + 2 :])


def from_everyone(x, axis):
    copies = jnp.broadcast_to(x, (lax.axis_size(axis), *x.shape))
    return lax.all_to_all(copies, axis, split_axis=0, concat_axis=0, tiled=True)


def collect(x, axis, dim):
    return in_order(from_everyone(x, axis), dim)


def total_of(x, axes):
    lines = x.reshape(-1, x.shape[-1])
    own = sent_and_summed(padded_to(lines, lax.axis_size(axes)), axes, 0)
    whole = collect(own, axes, 0)
    return whole[: len(lines)].reshape(x.shape)


def matmul(former, latter):
    return jnp.dot(former, latter, precision=HIGH, preferred_element_type=jnp.float32)


def contract_first(former, latter):
    return lax.dot_general(
        former, latter, (((0,), (0,)), ((), ())), precision=HIGH, preferred_element_type=jnp.float32
    )


def block_flags(structure_row, first_row, rows_count):
    position = first_row + jnp.arange(rows_count, dtype=jnp.int32)
    owners = position // BLK
    numbers = jnp.arange(structure_row.shape[0], dtype=jnp.int32)
    matches = (owners[:, None] == numbers[None, :]).astype(jnp.float32)
    return jnp.dot(matches, structure_row.astype(jnp.float32), precision=HIGH)


def body(front, structure, factor_front, factor_border, pivot_inverse):
    row_index = lax.axis_index(ROW)
    col_index = lax.axis_index("col")
    rows_here = front.shape[0]
    cols_here = front.shape[1]
    width_here = pivot_inverse.shape[1]
    supers = structure.shape[0]
    row_first = row_index * rows_here
    col_first = col_index * cols_here
    fetched = lax.all_gather(factor_front, "col", axis=2, tiled=True)
    fronts = []
    parents = []
    diagonals = []
    previous = None
    diag_prev = None
    for section in range(supers):
        gathered = fetched[section]
        row_flags = block_flags(structure[section], row_first, rows_here)
        factor_rows = gathered * row_flags[:, None]
        own_half = lax.dynamic_slice_in_dim(factor_rows, col_index % 2 * cols_here, cols_here, 0)
        factor_cols = broadcast_by_axis(own_half, ROW, col_index // 2)
        partial_value = contract_first(factor_rows, front)
        if section > 0:
            border = factor_border[section - 1]
            border_rows = lax.dynamic_slice_in_dim(border, row_index * width_here, width_here, 0)
            partial_value = partial_value + contract_first(border_rows, previous)
            parent_part = total_of(matmul(previous, factor_cols), "col")
            parent_rows = parent_part + matmul(diag_prev, border)
            parent_all = lax.all_gather(parent_rows, ROW, axis=0, tiled=True)
            parents.append(-parent_rows)
        image_rows = sent_and_summed(partial_value, ROW, 0)
        col_flags = block_flags(structure[section], col_first, cols_here)
        current = -(image_rows * col_flags[None, :])
        gram_rows = total_of(matmul(image_rows, factor_cols), "col")
        diag_now = pivot_inverse[section] + gram_rows
        if section > 0:
            parent_slice = lax.dynamic_slice_in_dim(
                parent_all, row_index * width_here, width_here, 1
            )
            diag_now = diag_now + contract_first(parent_slice, border)
        fronts.append(current)
        diagonals.append(diag_now)
        previous = current
        diag_prev = diag_now
    return (jnp.stack(fronts), jnp.stack(parents), jnp.stack(diagonals))


def solution(mesh):
    torus = Mesh(mesh.devices.reshape(8, 2, mesh.shape["col"]), ("row_0", "row_1", "col"))
    return jax.shard_map(
        body,
        mesh=torus,
        in_specs=(P(ROW, "col"), P(), P(None, ROW, "col"), P(), P(None, ROW, None)),
        out_specs=(P(None, ROW, "col"), P(None, ROW, None), P(None, ROW, None)),
        check_vma=False,
    )
```

profile of v0, /device:TPU:1, one launch (start us, length us, event | category | flops | bytes accessed | tf_op | source)
XLA Modules:
  0.0 465.4 jit_solution(13938320989205049159)
XLA Ops:
  11.3 91.5 %all-gather.4.cloned.1.call-done = f32[3,768,512]{1,2,0:T(8,128)} async-done(((f32[3,768,16]{1,2,0:T(8,128)}), f32[3,768,512]{1,2,0:T(8,128)}) %all-gather.4.cloned.1.call-update) | async-done | bytes 4718608 | tf_op jit(solution)/shard_map/all_gather | solution.py:89
  108.1 87.4 %all-reduce.5.cloned.1.call-done = (f32[384,512]{0,1:T(8,128)}, f32[384,512]{0,1:T(8,128)}, f32[384,512]{0,1:T(8,128)}) async-done(((f32[384,512]{0,1:T(8,128)}, f32[384,512]{0,1:T(8,128)}, f32[384,512]{0,1:T(8,128)}), (f32[384,512]{0,1:T(8,128)}, f32[384,512]{0,1:T(8,128)}, f32[384,512]{0,1:T(8,128)})) %all-reduce.5.cloned.1.call-update) | async-done | bytes 2359312 | tf_op jit(solution)/shard_map/psum | solution.py:17
  195.5 3.6 fusion.3
  199.1 8.3 %all-to-all-start = ((f32[16,32,384]{2,1,0:T(8,128)}), f32[16,32,384]{2,1,0:T(8,128)}, u32[]{:S(2)}, u32[]{:S(2)}) async-start(f32[16,32,384]{2,1,0:T(8,128)} %fusion.3), calls=%async_computation | async-start | bytes 1572864 | tf_op jit(solution)/shard_map/all_to_all | solution.py:29
  207.8 22.4 %all-to-all-done = f32[16,32,384]{2,1,0:T(8,128)} async-done(((f32[16,32,384]{2,1,0:T(8,128)}), f32[16,32,384]{2,1,0:T(8,128)}, u32[]{:S(2)}, u32[]{:S(2)}) %all-to-all-start) | async-done | bytes 786464 | tf_op jit(solution)/shard_map/all_to_all | solution.py:29
  231.4 8.4 %all-reduce.7.cloned.1.call-done = (f32[384,512]{0,1:T(8,128)}, f32[384,512]{0,1:T(8,128)}, f32[384,512]{0,1:T(8,128)}) async-done(((f32[384,512]{0,1:T(8,128)}, f32[384,512]{0,1:T(8,128)}, f32[384,512]{0,1:T(8,128)}), (f32[384,512]{0,1:T(8,128)}, f32[384,512]{0,1:T(8,128)}, f32[384,512]{0,1:T(8,128)})) %all-reduce.7.cloned.1.call-update) | async-done | bytes 2359312 | tf_op jit(solution)/shard_map/psum | solution.py:17
  242.5 8.3 %all-to-all-start.5 = ((f32[32,1,512]{2,1,0:T(1,128)}), f32[32,1,512]{2,1,0:T(1,128)S(1)}, u32[]{:S(2)}, u32[]{:S(2)}) async-start(f32[32,1,512]{2,1,0:T(1,128)} %copy.9), calls=%async_computation.5 | async-start | bytes 131072 | tf_op jit(solution)/shard_map/all_to_all | solution.py:29
  253.4 6.2 %all-to-all-done.5 = f32[32,1,512]{2,1,0:T(1,128)S(1)} async-done(((f32[32,1,512]{2,1,0:T(1,128)}), f32[32,1,512]{2,1,0:T(1,128)S(1)}, u32[]{:S(2)}, u32[]{:S(2)}) %all-to-all-start.5) | async-done | bytes 65568 | tf_op jit(solution)/shard_map/all_to_all | solution.py:29
  259.6 3.9 all-to-all-start.3
  265.1 7.3 %all-to-all-done.3 = f32[32,1,512]{2,1,0:T(1,128)S(1)} async-done(((f32[32,1,512]{2,1,0:T(1,128)}), f32[32,1,512]{2,1,0:T(1,128)S(1)}, u32[]{:S(2)}, u32[]{:S(2)}) %all-to-all-start.3) | async-done | bytes 65568 | tf_op jit(solution)/shard_map/all_to_all | solution.py:29
  273.0 3.9 all-to-all-start.6
  279.5 6.2 %all-to-all-done.6 = f32[32,1,512]{2,1,0:T(1,128)S(1)} async-done(((f32[32,1,512]{2,1,0:T(1,128)}), f32[32,1,512]{2,1,0:T(1,128)S(1)}, u32[]{:S(2)}, u32[]{:S(2)}) %all-to-all-start.6) | async-done | bytes 65568 | tf_op jit(solution)/shard_map/all_to_all | solution.py:48
  286.4 3.9 all-to-all-start.4
  290.3 5.1 %convolution_add_fusion.1 = f32[512,384]{1,0:T(8,128)} fusion(f32[512,384]{1,0:T(8,128)} %fusion.21, f32[768,512]{0,1:T(8,128)} %copy-done.3, f32[768,384]{1,0:T(8,128)S(1)} %copy-done), kind=kOutput, calls=%fused_computation.7 | convolution fusion | flops 1812135936 | bytes 4325376 | tf_op jit(solution)/shard_map/dot_general | solution.py:67
  295.4 3.7 all-to-all-done.4
  299.1 12.6 %all-to-all-start.1 = ((f32[16,32,384]{2,1,0:T(8,128)}), f32[16,32,384]{2,1,0:T(8,128)}, u32[]{:S(2)}, u32[]{:S(2)}) async-start(f32[16,32,384]{2,1,0:T(8,128)} %bitcast.123), calls=%async_computation.1 | async-start | bytes 1572864 | tf_op jit(solution)/shard_map/all_to_all | solution.py:29
  315.4 19.6 %all-to-all-done.1 = f32[16,32,384]{2,1,0:T(8,128)} async-done(((f32[16,32,384]{2,1,0:T(8,128)}), f32[16,32,384]{2,1,0:T(8,128)}, u32[]{:S(2)}, u32[]{:S(2)}) %all-to-all-start.1) | async-done | bytes 786464 | tf_op jit(solution)/shard_map/all_to_all | solution.py:29
  338.9 4.1 all-to-all-start.7
  345.7 6.2 %all-to-all-done.7 = f32[32,1,512]{2,1,0:T(1,128)S(1)} async-done(((f32[32,1,512]{2,1,0:T(1,128)}), f32[32,1,512]{2,1,0:T(1,128)S(1)}, u32[]{:S(2)}, u32[]{:S(2)}) %all-to-all-start.7) | async-done | bytes 65568 | tf_op jit(solution)/shard_map/all_to_all | solution.py:29
  352.5 3.9 all-to-all-start.9
  357.3 8.5 %all-to-all-done.9 = f32[32,1,512]{2,1,0:T(1,128)S(1)} async-done(((f32[32,1,512]{2,1,0:T(1,128)}), f32[32,1,512]{2,1,0:T(1,128)S(1)}, u32[]{:S(2)}, u32[]{:S(2)}) %all-to-all-start.9) | async-done | bytes 65568 | tf_op jit(solution)/shard_map/all_to_all | solution.py:29
  366.4 3.9 all-to-all-start.8
  373.8 5.4 %all-to-all-done.8 = f32[32,1,512]{2,1,0:T(1,128)S(1)} async-done(((f32[32,1,512]{2,1,0:T(1,128)}), f32[32,1,512]{2,1,0:T(1,128)S(1)}, u32[]{:S(2)}, u32[]{:S(2)}) %all-to-all-start.8) | async-done | bytes 65568 | tf_op jit(solution)/shard_map/all_to_all | solution.py:48
  379.9 4.6 all-to-all-start.10
  384.4 5.1 %convolution_add_fusion = f32[512,384]{1,0:T(8,128)} fusion(f32[512,384]{1,0:T(8,128)} %fusion.19, f32[768,512]{0,1:T(8,128)} %copy-done.2, f32[768,384]{1,0:T(8,128)S(1)} %copy-done), kind=kOutput, calls=%fused_computation.6 | convolution fusion | flops 1812135936 | bytes 4325376 | tf_op jit(solution)/shard_map/dot_general | solution.py:67
  389.6 3.8 all-to-all-done.10
  393.4 7.4 %all-to-all-start.2 = ((f32[16,32,384]{2,1,0:T(8,128)}), f32[16,32,384]{2,1,0:T(8,128)}, u32[]{:S(2)}, u32[]{:S(2)}) async-start(f32[16,32,384]{2,1,0:T(8,128)} %bitcast.122), calls=%async_computation.2 | async-start | bytes 1572864 | tf_op jit(solution)/shard_map/all_to_all | solution.py:29
  406.8 17.4 %all-to-all-done.2 = f32[16,32,384]{2,1,0:T(8,128)} async-done(((f32[16,32,384]{2,1,0:T(8,128)}), f32[16,32,384]{2,1,0:T(8,128)}, u32[]{:S(2)}, u32[]{:S(2)}) %all-to-all-start.2) | async-done | bytes 786464 | tf_op jit(solution)/shard_map/all_to_all | solution.py:29
  428.0 4.6 all-to-all-start.11
  434.1 7.3 %all-to-all-done.11 = f32[32,1,512]{2,1,0:T(1,128)} async-done(((f32[32,1,512]{2,1,0:T(1,128)}), f32[32,1,512]{2,1,0:T(1,128)}, u32[]{:S(2)}, u32[]{:S(2)}) %all-to-all-start.11) | async-done | bytes 65568 | tf_op jit(solution)/shard_map/all_to_all | solution.py:29
  442.9 4.5 all-to-all-start.12
  449.0 7.4 %all-to-all-done.12 = f32[32,1,512]{2,1,0:T(1,128)} async-done(((f32[32,1,512]{2,1,0:T(1,128)}), f32[32,1,512]{2,1,0:T(1,128)}, u32[]{:S(2)}, u32[]{:S(2)}) %all-to-all-start.12) | async-done | bytes 65568 | tf_op jit(solution)/shard_map/all_to_all | solution.py:48
  (86 shorter events, 54.8 us)
Async XLA Ops:
  7.2 188.4 %copy-start = (f32[768,384]{1,0:T(8,128)S(1)}, f32[768,384]{1,0:T(8,128)}, u32[]{:S(2)}) copy-start(f32[768,384]{1,0:T(8,128)} %param.5) | copy-start | bytes 3538948
  7.2 95.6 %all-gather.4.cloned.1.call-start = ((), (), s32[]{:S(2)}) async-start(), calls=%async_computation.13 | async-start | bytes 4866048 | tf_op jit(solution)/shard_map/all_gather | solution.py:89
  7.9 187.6 %all-reduce.5.cloned.1.call-start = ((), (), s32[]{:S(2)}) async-start(), calls=%async_computation.16 | async-start | bytes 4718592 | tf_op jit(solution)/shard_map/psum | solution.py:17
  105.6 2.4 copy-start.2
  105.6 2.4 copy-start.3
  108.0 131.8 %all-reduce.7.cloned.1.call-start = ((), (), s32[]{:S(2)}) async-start(), calls=%async_computation.17 | async-start | bytes 4718592 | tf_op jit(solution)/shard_map/psum | solution.py:17
  199.1 8.3 %copy-start.11 = (s32[3,96]{1,0:T(4,128)S(1)}, s32[3,96]{1,0:T(4,128)}, u32[]{:S(2)}) copy-start(s32[3,96]{1,0:T(4,128)} %param.6) | copy-start | bytes 3460
  199.1 31.1 %all-to-all-start = ((f32[16,32,384]{2,1,0:T(8,128)}), f32[16,32,384]{2,1,0:T(8,128)}, u32[]{:S(2)}, u32[]{:S(2)}) async-start(f32[16,32,384]{2,1,0:T(8,128)} %fusion.3), calls=%async_computation | async-start | bytes 1572864 | tf_op jit(solution)/shard_map/all_to_all | solution.py:29
  207.8 55.7 %copy-start.1 = (f32[2,512,512]{2,1,0:T(8,128)S(1)}, f32[2,512,512]{2,1,0:T(8,128)}, u32[]{:S(2)}) copy-start(f32[2,512,512]{2,1,0:T(8,128)} %param.8) | copy-start | bytes 6291460
  242.5 17.1 %all-to-all-start.5 = ((f32[32,1,512]{2,1,0:T(1,128)}), f32[32,1,512]{2,1,0:T(1,128)S(1)}, u32[]{:S(2)}, u32[]{:S(2)}) async-start(f32[32,1,512]{2,1,0:T(1,128)} %copy.9), calls=%async_computation.5 | async-start | bytes 131072 | tf_op jit(solution)/shard_map/all_to_all | solution.py:29
  259.6 12.7 %all-to-all-start.3 = ((f32[32,1,512]{2,1,0:T(1,128)}), f32[32,1,512]{2,1,0:T(1,128)S(1)}, u32[]{:S(2)}, u32[]{:S(2)}) async-start(f32[32,1,512]{2,1,0:T(1,128)} %copy.8), calls=%async_computation.3 | async-start | bytes 131072 | tf_op jit(solution)/shard_map/all_to_all | solution.py:29
  273.0 12.7 %all-to-all-start.6 = ((f32[32,1,512]{2,1,0:T(1,128)}), f32[32,1,512]{2,1,0:T(1,128)S(1)}, u32[]{:S(2)}, u32[]{:S(2)}) async-start(f32[32,1,512]{2,1,0:T(1,128)} %broadcast_in_dim.11), calls=%async_computation.6 | async-start | bytes 131072 | tf_op jit(solution)/shard_map/all_to_all | solution.py:48
  286.4 12.7 %all-to-all-start.4 = ((f32[32,1,512]{2,1,0:T(1,128)}), f32[32,1,512]{2,1,0:T(1,128)S(1)}, u32[]{:S(2)}, u32[]{:S(2)}) async-start(f32[32,1,512]{2,1,0:T(1,128)} %broadcast_in_dim.10), calls=%async_computation.4 | async-start | bytes 131072 | tf_op jit(solution)/shard_map/all_to_all | solution.py:48
  299.1 12.6 %copy-start.7 = (f32[32,1,512]{2,1,0:T(1,128)}, f32[32,1,512]{2,1,0:T(1,128)S(1)}, u32[]{:S(2)}) copy-start(f32[32,1,512]{2,1,0:T(1,128)S(1)} %all-to-all-done.4) | copy-start | bytes 196612
  299.1 35.9 %all-to-all-start.1 = ((f32[16,32,384]{2,1,0:T(8,128)}), f32[16,32,384]{2,1,0:T(8,128)}, u32[]{:S(2)}, u32[]{:S(2)}) async-start(f32[16,32,384]{2,1,0:T(8,128)} %bitcast.123), calls=%async_computation.1 | async-start | bytes 1572864 | tf_op jit(solution)/shard_map/all_to_all | solution.py:29
  311.7 89.1 %all-gather.6.cloned.1.call-start = ((), (), s32[]{:S(2)}) async-start(), calls=%async_computation.14 | async-start | bytes 1114112 | tf_op jit(solution)/shard_map/all_gather | solution.py:108
  338.9 13.0 %all-to-all-start.7 = ((f32[32,1,512]{2,1,0:T(1,128)}), f32[32,1,512]{2,1,0:T(1,128)S(1)}, u32[]{:S(2)}, u32[]{:S(2)}) async-start(f32[32,1,512]{2,1,0:T(1,128)} %copy.10), calls=%async_computation.7 | async-start | bytes 131072 | tf_op jit(solution)/shard_map/all_to_all | solution.py:29
  351.9 0.6 copy-start.9
  352.5 13.3 %all-to-all-start.9 = ((f32[32,1,512]{2,1,0:T(1,128)}), f32[32,1,512]{2,1,0:T(1,128)S(1)}, u32[]{:S(2)}, u32[]{:S(2)}) async-start(f32[32,1,512]{2,1,0:T(1,128)} %copy.11), calls=%async_computation.9 | async-start | bytes 131072 | tf_op jit(solution)/shard_map/all_to_all | solution.py:29
  365.8 0.7 copy-start.8
  366.4 12.7 %all-to-all-start.8 = ((f32[32,1,512]{2,1,0:T(1,128)}), f32[32,1,512]{2,1,0:T(1,128)S(1)}, u32[]{:S(2)}, u32[]{:S(2)}) async-start(f32[32,1,512]{2,1,0:T(1,128)} %broadcast_in_dim.12), calls=%async_computation.8 | async-start | bytes 131072 | tf_op jit(solution)/shard_map/all_to_all | solution.py:48
  379.9 13.5 %all-to-all-start.10 = ((f32[32,1,512]{2,1,0:T(1,128)}), f32[32,1,512]{2,1,0:T(1,128)}, u32[]{:S(2)}, u32[]{:S(2)}) async-start(f32[32,1,512]{2,1,0:T(1,128)} %broadcast_in_dim.13), calls=%async_computation.10 | async-start | bytes 131072 | tf_op jit(solution)/shard_map/all_to_all | solution.py:48
  393.4 30.7 %all-to-all-start.2 = ((f32[16,32,384]{2,1,0:T(8,128)}), f32[16,32,384]{2,1,0:T(8,128)}, u32[]{:S(2)}, u32[]{:S(2)}) async-start(f32[16,32,384]{2,1,0:T(8,128)} %bitcast.122), calls=%async_computation.2 | async-start | bytes 1572864 | tf_op jit(solution)/shard_map/all_to_all | solution.py:29
  400.8 55.6 %all-gather.8.cloned.1.call-start = ((), (), s32[]{:S(2)}) async-start(), calls=%async_computation.15 | async-start | bytes 1114112 | tf_op jit(solution)/shard_map/all_gather | solution.py:108
  402.6 0.6 copy-start.5
  404.6 42.9 %copy-start.4 = (f32[32,512]{1,0:T(8,128)S(1)}, f32[32,512]{1,0:T(8,128)}, u32[]{:S(2)}) copy-start(f32[32,512]{1,0:T(8,128)} %convolution_add_fusion.3) | copy-start | bytes 196612
  406.7 25.8 %copy-start.10 = (f32[384]{0:T(512)S(1)}, f32[384]{0:T(512)}, u32[]{:S(2)}) copy-start(f32[384]{0:T(512)} %convolution_reduce_fusion.3) | copy-start | bytes 4612
  427.3 30.9 %copy-start.6 = (f32[32,512]{1,0:T(8,128)S(1)}, f32[32,512]{1,0:T(8,128)}, u32[]{:S(2)}) copy-start(f32[32,512]{1,0:T(8,128)} %copy-done.5) | copy-start | bytes 196612
  428.0 13.4 %all-to-all-start.11 = ((f32[32,1,512]{2,1,0:T(1,128)}), f32[32,1,512]{2,1,0:T(1,128)}, u32[]{:S(2)}, u32[]{:S(2)}) async-start(f32[32,1,512]{2,1,0:T(1,128)} %copy.12), calls=%async_computation.11 | async-start | bytes 131072 | tf_op jit(solution)/shard_map/all_to_all | solution.py:29
  442.9 13.5 %all-to-all-start.12 = ((f32[32,1,512]{2,1,0:T(1,128)}), f32[32,1,512]{2,1,0:T(1,128)}, u32[]{:S(2)}, u32[]{:S(2)}) async-start(f32[32,1,512]{2,1,0:T(1,128)} %broadcast_in_dim.14), calls=%async_computation.12 | async-start | bytes 131072 | tf_op jit(solution)/shard_map/all_to_all | solution.py:48
Sparse Core Ops, SparseCore 0:
  11.2 91.5 all-gather.3
  108.1 87.3 all-reduce.4
  198.6 41.2 all-reduce.6
  315.2 39.2 all-gather.5
  404.7 38.7 all-gather.7
where the time goes:
time: 467 us; the launch traced here: 465 us
  waiting for transfers between devices  310 us (66%)
  starting transfers between devices  74.1 us (16%)
  matrix products  40.5 us (9%)
  other arithmetic  17.4 us (4%)
  between operations  14.1 us (3%)
  local copies, waits for them, and re-layouts  9.62 us (2%)
    psum x2, waiting for transfers between devices, broadcast_by_axis(): x = lax.psum(x, axis)  95.9 us
    all_to_all x8, waiting for transfers between devices, sent_and_summed(): pieces = lax.all_to_all(split_up(x, dim, length), axis, 0, 0, tiled=True)  94.9 us
    all_gather x1, waiting for transfers between devices, body(): fetched = lax.all_gather(factor_front, 'col', axis=2, tiled=True)  91.5 us
    all_to_all x8, starting transfers between devices, sent_and_summed(): pieces = lax.all_to_all(split_up(x, dim, length), axis, 0, 0, tiled=True)  53 us
    all_to_all x5, waiting for transfers between devices, from_everyone(): return lax.all_to_all(copies, axis, split_axis=0, concat_axis=0, tiled=True)  26.6 us
    dot_general x7, matrix products, contract_first(): lax.dot_general(former, latter, (((0,), (0,)), ((), ())), precision=HIGH,...  22.4 us
    all_to_all x5, starting transfers between devices, from_everyone(): return lax.all_to_all(copies, axis, split_axis=0, concat_axis=0, tiled=True)  20.7 us
    dot_general x7, matrix products, matmul(): jnp.dot(former, latter, precision=HIGH, preferred_element_type=jnp.float32)  13.3 us
  transfers between devices with their start and end apart: 18, of which 16 were waited for; matrix products, arithmetic and copies ran while one was open for 12% of the time, Pallas kernels for 0%

commit v1 on v0

v1 whole, which is shorter than its diff:
```python
import functools

import jax
import jax.numpy as jnp
from jax import lax
from jax.experimental import pallas as pl
from jax.experimental.pallas import tpu as pltpu
from jax.sharding import PartitionSpec as P

NX, NY, NZ = 4, 8, 8
SIZES = (NX, NY)
SUPER = 3
BLK = 128
PIECES = 4
AG_DELAY = (0, 3, 6)
BC_START = (0, 6, 12)
MESH = pl.DeviceIdType.MESH
F32 = jnp.float32


def gather_plan():
    msgs = []
    for first in range(2):
        n1, n2 = SIZES[first], SIZES[1 - first]
        for j in range(1, n1 // 2 + 1):
            for s in (1, -1):
                msgs.append((j, first, s, j, None, 0))
        for o in range(-(n1 // 2) + 1, n1 // 2 + 1):
            for i in range(1, n2 // 2 + 1):
                for s in (1, -1):
                    msgs.append((abs(o) + i, first, 0, o, s, i))
    return msgs


MSGS = gather_plan()
INDEX = {m[1:]: i for i, m in enumerate(MSGS)}
BY_KEY = {m[1:]: m for m in MSGS}


def wrap(v, n):
    return lax.rem(v + n, n)


def split(v):
    high = v.astype(jnp.bfloat16)
    low = (v - high.astype(F32)).astype(jnp.bfloat16)
    return high, low


NN = (((1,), (0,)), ((), ()))
NT = (((1,), (1,)), ((), ()))


def dot3(a, b, dims=NN):
    def one(p, q):
        return lax.dot_general(p, q, dims, preferred_element_type=F32)
    return one(a[0], b[0]) + (one(a[0], b[1]) + one(a[1], b[0]))


def kernel(flag_ref, a_ref, f_ref, b_ref, p_ref, x_out, par_out, d_out,
           FA, FB, PF, Yp, E, RB, Hc, Ah, Al, Bh, Bl, BTh, BTl, Hh, Hl, Yr, TP, R1, R2, R3, TF, U, Q,
           ag_s, ag_r, pz_s, pz_r, ex_s, ex_r, rs_s, rs_r, bc_s, bc_r, rt_s, rt_r, sx_s, sx_r, cp_s,
           t1_s, t1_r, t2_s, t2_r, t3_s, t3_r):
    row = lax.axis_index("row")
    col = lax.axis_index("col")
    z, core = lax.div(row, 2), lax.rem(row, 2)
    x, y = lax.div(col, NY), lax.rem(col, NY)
    other = 1 - core

    def at(dx=0, dy=0, dz=0):
        return (wrap(z + dz, NZ) * 2 + core, wrap(x + dx, NX) * NY + wrap(y + dy, NY))

    sibling = (z * 2 + other, col)

    def remote(src, dst, s_sem, r_sem, dev):
        return pltpu.make_async_remote_copy(
            src_ref=src, dst_ref=dst, send_sem=s_sem, recv_sem=r_sem, device_id=dev, device_id_type=MESH)

    sends = []

    def start(c):
        c.start()
        sends.append(c)

    barrier = pltpu.get_barrier_semaphore()
    peers = [at(dx=o) for o in range(1, NX)] + [at(dy=o) for o in range(1, NY)]
    peers += [at(dz=1), at(dz=-1), sibling]
    for dev in peers:
        pl.semaphore_signal(barrier, inc=1, device_id=dev, device_id_type=MESH)

    for k in range(SUPER):
        for j in range(6):
            flag = flag_ref[k, row * 6 + j].astype(F32)
            dst = (FA, FB)[j // 3]
            dst[k, x, y, :, (j % 3) * BLK:(j % 3 + 1) * BLK] = f_ref[k, :, j * BLK:(j + 1) * BLK] * flag
    PF[:, z, core] = p_ref[0:2]
    pl.semaphore_wait(barrier, len(peers))

    def ag_copy(k, key, back):
        first, s1, o, s2, i = key
        n1, n2 = SIZES[first], SIZES[1 - first]
        F = (FA, FB)[first]
        if s2 is None:
            half, s = o == n1 // 2, s1
            off1, off2 = -s1 * (o - 1 + back), 0
            step = (s, 0)
        else:
            half, s = i == n2 // 2, s2
            off1, off2 = o, -s2 * (i - 1 + back)
            step = (0, s)
        rows = pl.ds(0 if s > 0 else 8, 8) if half else pl.ds(0, 16)
        if first == 1:
            off1, off2 = off2, off1
            step = step[::-1]
        ref = F.at[k, wrap(x + off1, NX), wrap(y + off2, NY), rows]
        n = k * len(MSGS) + INDEX[key]
        return remote(ref, ref, ag_s.at[n], ag_r.at[n], at(*step))

    def ag_second(k, first, o):
        o = o if o > -(SIZES[first] // 2) else -o
        for s in (1, -1):
            start(ag_copy(k, (first, 0, o, s, 1), 0))

    def ag_begin(k):
        for first in range(2):
            for s in (1, -1):
                start(ag_copy(k, (first, s, 1, None, 0), 0))
        for first in range(2):
            ag_second(k, first, 0)

    def ag_arrive(k, m):
        key = m[1:]
        ag_copy(k, key, 1).wait_recv()
        first, s1, o, s2, i = key
        n1, n2 = SIZES[first], SIZES[1 - first]
        if s2 is None:
            if o < n1 // 2:
                start(ag_copy(k, (first, s1, o + 1, None, 0), 0))
                ag_second(k, first, -s1 * o)
            elif s1 < 0:
                ag_second(k, first, o)
        elif i < n2 // 2:
            start(ag_copy(k, (first, 0, o, s2, i + 1), 0))

    def ag_tick(k, t):
        for m in sorted((m for m in MSGS if m[0] == t), key=lambda m: (m[4] is not None, m[5])):
            ag_arrive(k, m)

    def pz_copy(s, t, back):
        half = t == NZ // 2
        rows = pl.ds(0 if s > 0 else 16, 16) if half else pl.ds(0, 32)
        ref = PF.at[:, wrap(z - s * (t - 1 + back), NZ), core, rows]
        n = (t - 1) * 2 + (s > 0)
        return remote(ref, ref, pz_s.at[n], pz_r.at[n], at(dz=s))

    def pz_tick(t):
        for s in (1, -1):
            if t > 0:
                pz_copy(s, t, 1).wait_recv()
            if t < NZ // 2:
                start(pz_copy(s, t + 1, 0))

    def pz_pair(side):
        ref = PF.at[:, :, side]
        return remote(ref, ref, pz_s.at[8], pz_r.at[8], sibling)

    def prepare():
        Ah[...], Al[...] = split(a_ref[...])
        for i in range(2):
            b = b_ref[i]
            Bh[i], Bl[i] = split(b)
            BTh[i], BTl[i] = split(b.T)

    def product(k):
        for h in range(2):
            out = None
            for F, base in ((FA, 0), (FB, 384)):
                left = split(F[k, 2 * h:2 * h + 2].reshape(256, 384))
                term = dot3(left, (Ah[base:base + 384], Al[base:base + 384]))
                out = term if out is None else out + term
            if k > 0:
                rows = slice(h * 256, h * 256 + 256)
                before = split(Yp[k - 1].reshape(512, 384))
                out = out - dot3((BTh[k - 1, rows], BTl[k - 1, rows]), before)
            Yp[k, 4 * h:4 * h + 4] = out.reshape(4, 2, 32, 384)

    def ex_copy(k):
        return remote(Yp.at[k, :, other], E.at[k], ex_s.at[k], ex_r.at[k], sibling)

    def ex_finish(k):
        ex_copy(k).wait_recv()
        E[k] = E[k] + Yp[k, :, core]

    def rs_rows(s, t):
        return (pl.ds(0, 16) if s > 0 else pl.ds(16, 16)) if t == 1 else pl.ds(0, 32)

    def rs_copy(k, s, t):
        n = (k * 4 + t - 1) * 2 + (s > 0)
        rows = rs_rows(s, t)
        return remote(E.at[k, wrap(z + s * (5 - t), NZ), rows], RB.at[k, int(s > 0), t - 1, rows],
                      rs_s.at[n], rs_r.at[n], at(dz=s))

    def rs_tick(k, t):
        for s in (1, -1):
            if t > 0:
                rs_copy(k, s, t).wait_recv()
                rows = rs_rows(s, t)
                block = wrap(z + s * (4 - t), NZ)
                E[k, block, rows] = E[k, block, rows] + RB[k, int(s > 0), t - 1, rows]
            if t < 4:
                start(rs_copy(k, s, t + 1))

    def columns_out(k):
        image = E[k, z]
        Yr[k] = image
        for j in range(3):
            flag = flag_ref[k, col * 3 + j].astype(F32)
            lanes = slice(j * BLK, (j + 1) * BLK)
            x_out[k, :, lanes] = -(image[:, lanes] * flag)

    root_z = lax.div(col, 4)
    root_core = lax.rem(lax.div(col, 2), 2)
    in_root_plane = z == root_z
    is_root = jnp.logical_and(in_root_plane, core == root_core)
    even = lax.rem(col, 2) == 0

    def root_copies(k):
        for F, mine in ((FA, even), (FB, jnp.logical_not(even))):
            yield (pltpu.make_async_copy(F.at[k], Hc.at[k], cp_s.at[k]),
                   remote(F.at[k], Hc.at[k], rt_s.at[k], rt_r.at[k], sibling),
                   jnp.logical_and(is_root, mine))

    def bc_root(k):
        for local, away, here in root_copies(k):
            @pl.when(here)
            def _():
                away.start()
                local.start()
                local.wait()

        @pl.when(jnp.logical_and(in_root_plane, core != root_core))
        def _():
            remote(Hc.at[k], Hc.at[k], rt_s.at[k], rt_r.at[k], sibling).wait_recv()

    def bc_root_done(k):
        for local, away, here in root_copies(k):
            @pl.when(here)
            def _():
                away.wait_send()

    def bc_copy(k, s, p):
        n = (k * 2 + (s > 0)) * PIECES + p
        w = NY // PIECES
        ref = Hc.at[k, 2 * core + (s > 0), pl.ds(p * w, w)]
        return remote(ref, ref, bc_s.at[n], bc_r.at[n], at(dz=s))

    def bc_place(s):
        return wrap(s * (z - root_z) + NZ, NZ)

    def bc_slot(slot):
        for k in range(SUPER):
            if not 0 <= slot - BC_START[k] < NZ - 1 + PIECES:
                continue
            for s in (1, -1):
                place = bc_place(s)
                p = slot - BC_START[k] - place
                there = jnp.logical_and(p >= 0, p < PIECES)

                @pl.when(jnp.logical_and(there, place > 0))
                def _():
                    bc_copy(k, s, p).wait_recv()

                @pl.when(jnp.logical_and(there, place < NZ - 1))
                def _():
                    bc_copy(k, s, p).start()

    def bc_done(k):
        for p in range(PIECES):
            for s in (1, -1):
                @pl.when(bc_place(s) < NZ - 1)
                def _():
                    bc_copy(k, s, p).wait_send()

    def bc_pair(k, side):
        ref = Hc.at[k, pl.ds(2 * side, 2)]
        return remote(ref, ref, sx_s.at[k], sx_r.at[k], sibling)

    def bc_swap(k):
        @pl.when(jnp.logical_not(in_root_plane))
        def _():
            bc_pair(k, core).start()

    def bc_swapped(k):
        @pl.when(jnp.logical_not(in_root_plane))
        def _():
            bc_pair(k, other).wait_recv()
            bc_pair(k, core).wait_send()

    def reduced_factor(k):
        h = Hc[k].reshape(512, 384)
        if k > 0:
            h = h - dot3((BTh[k - 1], BTl[k - 1]), (Hh[k - 1], Hl[k - 1]))
        Hh[k], Hl[k] = split(h)

    def gram(k):
        if k == 0:
            TP[0:32] = dot3(split(Yr[0]), (Hh[0], Hl[0]), NT)
        else:
            left = Yr[k - 1:k + 1].reshape(64, 384)
            TP[64 * k - 32:64 * k + 32] = dot3(split(left), (Hh[k], Hl[k]), NT)

    def piece_of(ref, at_y):
        return ref.at[pl.ds(pl.multiple_of(lax.div(at_y, 2) * 40, 8), 40),
                      pl.ds(pl.multiple_of(lax.rem(at_y, 2) * 256, 256), 256)]

    def t_sum():
        c1 = [remote(piece_of(TP, wrap(y + o, NY)), R1.at[o], t1_s.at[o], t1_r.at[o], at(dy=o)) for o in range(1, NY)]
        for c in c1:
            start(c)
        own = piece_of(TP, y)[...]
        for o in range(1, NY):
            c1[o - 1].wait_recv()
            own = own + R1[o]
        R2[0] = own
        c2 = [remote(R2.at[0], R2.at[o], t2_s.at[o], t2_r.at[o], at(dx=o)) for o in range(1, NX)]
        for c in c2:
            start(c)
        for c in c2:
            c.wait_recv()
        total = R2[wrap(x, NX)]
        for i in range(1, NX):
            total = total + R2[wrap(x - i + NX, NX)]
        R3[...] = total
        c3 = [remote(R3, piece_of(TF, y), t3_s.at[o], t3_r.at[o], at(dy=o)) for o in range(1, NY)]
        for c in c3:
            start(c)
        piece_of(TF, y)[...] = total
        for o in range(1, NY):
            piece = piece_of(TF, wrap(y - o, NY))
            remote(piece, piece, t3_s.at[o], t3_r.at[o], at(dy=o)).wait_recv()

    def pivot_terms():
        b0, b1 = (Bh[0], Bl[0]), (Bh[1], Bl[1])
        mine = pl.ds(pl.multiple_of(row * 32, 32), 32)
        bt0, bt1 = (BTh[0, mine], BTl[0, mine]), (BTh[1, mine], BTl[1, mine])
        p0, p1 = split(PF[0].reshape(512, 512)), split(PF[1].reshape(512, 512))
        own0, own1, own2 = p_ref[0], p_ref[1], p_ref[2]
        q1 = own1 + dot3(split(dot3(bt0, p0, NT)), b0)
        U[0] = dot3(split(own0), b0)
        U[1] = dot3(split(q1), b1)
        inner = dot3(split(dot3(split(dot3(bt1, b0, NT)), p0)), b0) + dot3(bt1, p1, NT)
        Q[0] = q1
        Q[1] = own2 + dot3(split(inner), b1)

    def ag_step(g):
        for k in range(SUPER):
            if g == AG_DELAY[k]:
                ag_begin(k)
            elif 0 < g - AG_DELAY[k] <= 6:
                ag_tick(k, g - AG_DELAY[k])

    def slots(*numbers):
        for n in numbers:
            bc_slot(n)

    ag_step(0)
    pz_tick(0)
    prepare()
    for g in range(1, 6):
        ag_step(g)
        if g <= 4:
            pz_tick(g)
        if g == 4:
            start(pz_pair(core))
    ag_step(6)
    bc_root(0)
    slots(0)
    product(0)
    start(ex_copy(0))
    slots(1, 2)
    ag_step(7)
    slots(3, 4)
    ex_finish(0)
    rs_tick(0, 0)
    ag_step(8)
    slots(5)
    rs_tick(0, 1)
    ag_step(9)
    bc_root(1)
    slots(6)
    product(1)
    start(ex_copy(1))
    slots(7)
    rs_tick(0, 2)
    ag_step(10)
    slots(8, 9)
    rs_tick(0, 3)
    ex_finish(1)
    rs_tick(1, 0)
    ag_step(11)
    slots(10, 11)
    rs_tick(0, 4)
    bc_swap(0)
    rs_tick(1, 1)
    ag_step(12)
    bc_root(2)
    slots(12)
    product(2)
    start(ex_copy(2))
    slots(13)
    rs_tick(1, 2)
    slots(14)
    ex_finish(2)
    rs_tick(2, 0)
    rs_tick(1, 3)
    columns_out(0)
    bc_swapped(0)
    reduced_factor(0)
    slots(15)
    rs_tick(2, 1)
    rs_tick(1, 4)
    slots(16)
    bc_swap(1)
    columns_out(1)
    gram(0)
    slots(17)
    rs_tick(2, 2)
    slots(18)
    bc_swapped(1)
    reduced_factor(1)
    slots(19)
    rs_tick(2, 3)
    slots(20)
    gram(1)
    slots(21)
    rs_tick(2, 4)
    slots(22)
    bc_swap(2)
    columns_out(2)
    pz_pair(other).wait_recv()
    pivot_terms()
    bc_swapped(2)
    reduced_factor(2)
    gram(2)
    t_sum()
    d_out[0] = p_ref[0] + TF[0:32]
    d_out[1] = Q[0] + TF[64:96]
    d_out[2] = Q[1] + TF[128:160]
    par_out[0] = TF[32:64] - U[0]
    par_out[1] = TF[96:128] - U[1]
    for c in sends:
        c.wait_send()
    for k in range(SUPER):
        bc_root_done(k)
        bc_done(k)


def body(front, structure, factor_front, factor_border, pivot_inverse):
    vmem = pl.BlockSpec(memory_space=pltpu.VMEM)
    dma = lambda n: pltpu.SemaphoreType.DMA((n,))
    v = lambda *shape: pltpu.VMEM(shape, F32)
    h = lambda *shape: pltpu.VMEM(shape, jnp.bfloat16)
    n_ag = SUPER * len(MSGS)
    return pl.pallas_call(
        kernel,
        out_shape=(
            jax.ShapeDtypeStruct((3, 32, 384), F32),
            jax.ShapeDtypeStruct((2, 32, 512), F32),
            jax.ShapeDtypeStruct((3, 32, 512), F32),
        ),
        in_specs=[pl.BlockSpec(memory_space=pltpu.SMEM)] + [vmem] * 4,
        out_specs=(vmem,) * 3,
        scratch_shapes=[
            v(3, NX, NY, 16, 384), v(3, NX, NY, 16, 384),
            v(2, NZ, 2, 32, 512),
            v(3, NZ, 2, 32, 384),
            v(3, NZ, 32, 384),
            v(3, 2, 4, 32, 384),
            v(3, NX, NY, 16, 384),
            h(768, 384), h(768, 384),
            h(2, 512, 512), h(2, 512, 512), h(2, 512, 512), h(2, 512, 512),
            h(3, 512, 384), h(3, 512, 384),
            v(3, 32, 384),
            v(160, 512),
            v(NY, 40, 256), v(NX, 40, 256), v(40, 256),
            v(160, 512),
            v(2, 32, 512), v(2, 32, 512),
            dma(n_ag), dma(n_ag),
            dma(9), dma(9),
            dma(3), dma(3),
            dma(24), dma(24),
            dma(6 * PIECES), dma(6 * PIECES),
            dma(3), dma(3),
            dma(3), dma(3),
            dma(3),
            dma(NY), dma(NY), dma(NX), dma(NX), dma(NY), dma(NY),
        ],
        compiler_params=pltpu.CompilerParams(
            collective_id=0, has_side_effects=True, vmem_limit_bytes=56 * 2**20),
        cost_estimate=pl.CostEstimate(flops=8 * 10**9, bytes_accessed=5 * 10**6, transcendentals=0),
    )(structure, front, jnp.transpose(factor_front, (0, 2, 1)), factor_border, pivot_inverse)


def solution(mesh):
    return jax.shard_map(
        body,
        mesh=mesh,
        in_specs=(P("row", "col"), P(), P(None, "row", "col"), P(), P(None, "row", None)),
        out_specs=(P(None, "row", "col"), P(None, "row", None), P(None, "row", None)),
        check_vma=False,
    )
```

time: 467 us -> 152 us (0.33)
  the two profiles are of different devices: /device:TPU:1 before, /device:TPU:2 now
where the time goes in v1:
time: 152 us
  Pallas kernels  147 us (97%)
  local copies, waits for them, and re-layouts  4.76 us (3%)
    pallas_call x1, Pallas kernels, body(): pl.pallas_call(kernel, out_shape=(jax.ShapeDtypeStruct((3, 32, 384), F32)...  147 us
    unnamed x3, local copies, waits for them, and re-layouts  4.76 us

profile of v1, /device:TPU:2, one launch (start us, length us, event | category | flops | bytes accessed | tf_op | source)
XLA Modules:
  0.0 151.9 jit_solution(4354946615289618284)
XLA Ops:
  0.6 146.5 %shard_map.76 = (f32[3,32,384]{2,1,0:T(8,128)}, f32[2,32,512]{2,1,0:T(8,128)}, f32[3,32,512]{2,1,0:T(8,128)}) custom-call(s32[3,96]{1,0:T(4,128)} %flag_ref.1, f32[768,384]{1,0:T(8,128)} %a_ref.1, f32[3,16,768]{2,1,0:T(8,128)} %bitcast.1, f32[2,512,512]{2,1,0:T(8,128)} %b_ref.1, f32[3,32,512]{2,1,0:T(8,128)} %p_ref.1), custom_call_target="tpu_custom_call" | custom-call | flops 8000000000 | bytes 5000000 | tf_op jit(solution)/shard_map/pallas_call | solution.py:464
  147.2 1.6 %copy.11 = f32[3,32,384]{2,1,0:T(8,128)} copy(f32[3,32,384]{2,1,0:T(8,128)} %get-tuple-element.6) | data formatting | bytes 294912
  148.8 1.6 %copy.12 = f32[2,32,512]{2,1,0:T(8,128)} copy(f32[2,32,512]{2,1,0:T(8,128)} %get-tuple-element.7) | data formatting | bytes 262144
  150.3 1.6 %copy.13 = f32[3,32,512]{2,1,0:T(8,128)} copy(f32[3,32,512]{2,1,0:T(8,128)} %get-tuple-element.8) | data formatting | bytes 393216

commit v2 on v1

v2 whole, which is shorter than its diff:
```python
import functools

import jax
import jax.numpy as jnp
from jax import lax
from jax.experimental import pallas as pl
from jax.experimental.pallas import tpu as pltpu
from jax.sharding import PartitionSpec as P

NX, NY, NZ = 4, 8, 8
SIZES = (NX, NY)
SUPER = 3
BLK = 128
OFFSETS = [(dx, dy) for dx in range(1 - NX // 2, NX // 2 + 1) for dy in range(1 - NY // 2, NY // 2 + 1)]
MESH = pl.DeviceIdType.MESH
F32 = jnp.float32


def gather_plan():
    msgs = []
    for first in range(2):
        n1, n2 = SIZES[first], SIZES[1 - first]
        for j in range(1, n1 // 2 + 1):
            for s in (1, -1):
                msgs.append((j, first, s, j, None, 0))
        for o in range(-(n1 // 2) + 1, n1 // 2 + 1):
            for i in range(1, n2 // 2 + 1):
                for s in (1, -1):
                    msgs.append((abs(o) + i, first, 0, o, s, i))
    return msgs


MSGS = gather_plan()
INDEX = {m[1:]: i for i, m in enumerate(MSGS)}
BY_KEY = {m[1:]: m for m in MSGS}


def wrap(v, n):
    return lax.rem(v + n, n)


def split(v):
    high = v.astype(jnp.bfloat16)
    low = (v - high.astype(F32)).astype(jnp.bfloat16)
    return high, low


NN = (((1,), (0,)), ((), ()))
NT = (((1,), (1,)), ((), ()))


def dot3(a, b, dims=NN):
    def one(p, q):
        return lax.dot_general(p, q, dims, preferred_element_type=F32)
    return one(a[0], b[0]) + (one(a[0], b[1]) + one(a[1], b[0]))


def kernel(flag_ref, a_ref, f_ref, b_ref, p_ref, x_out, par_out, d_out,
           FA, FB, PF, Yp, E, RB, Hc, Ah, Al, Bh, Bl, BTh, BTl, Hh, Hl, Yr, TP, R1, R2, R3, TF, U, Q,
           ag_s, ag_r, pz_s, pz_r, ex_s, ex_r, rs_s, rs_r, bc_s, bc_r, rt_s, rt_r, sx_s, sx_r, cp_s,
           t1_s, t1_r, t2_s, t2_r):
    row = lax.axis_index("row")
    col = lax.axis_index("col")
    z, core = lax.div(row, 2), lax.rem(row, 2)
    x, y = lax.div(col, NY), lax.rem(col, NY)
    other = 1 - core

    def at(dx=0, dy=0, dz=0):
        return (wrap(z + dz, NZ) * 2 + core, wrap(x + dx, NX) * NY + wrap(y + dy, NY))

    sibling = (z * 2 + other, col)

    def remote(src, dst, s_sem, r_sem, dev):
        return pltpu.make_async_remote_copy(
            src_ref=src, dst_ref=dst, send_sem=s_sem, recv_sem=r_sem, device_id=dev, device_id_type=MESH)

    sends = []

    def start(c):
        c.start()
        sends.append(c)

    barrier = pltpu.get_barrier_semaphore()
    peers = [(row, wrap(col + o, NX * NY)) for o in range(1, NX * NY)]
    peers += [at(dz=1), at(dz=-1), sibling]
    for dev in peers:
        pl.semaphore_signal(barrier, inc=1, device_id=dev, device_id_type=MESH)

    for k in range(SUPER):
        for j in range(6):
            flag = flag_ref[k, row * 6 + j].astype(F32)
            dst = (FA, FB)[j // 3]
            dst[k, x, y, :, (j % 3) * BLK:(j % 3 + 1) * BLK] = f_ref[k, :, j * BLK:(j + 1) * BLK] * flag
    PF[:, z, core] = p_ref[0:2]
    TP[96:128] = jnp.zeros((32, 512), F32)
    pl.semaphore_wait(barrier, len(peers))

    def ag_copy(key, back):
        first, s1, o, s2, i = key
        n1, n2 = SIZES[first], SIZES[1 - first]
        F = (FA, FB)[first]
        if s2 is None:
            half, s = o == n1 // 2, s1
            off1, off2 = -s1 * (o - 1 + back), 0
            step = (s, 0)
        else:
            half, s = i == n2 // 2, s2
            off1, off2 = o, -s2 * (i - 1 + back)
            step = (0, s)
        rows = pl.ds(0 if s > 0 else 8, 8) if half else pl.ds(0, 16)
        if first == 1:
            off1, off2 = off2, off1
            step = step[::-1]
        ref = F.at[:, wrap(x + off1, NX), wrap(y + off2, NY), rows]
        n = INDEX[key]
        return remote(ref, ref, ag_s.at[n], ag_r.at[n], at(*step))

    def ag_second(first, o):
        o = o if o > -(SIZES[first] // 2) else -o
        for s in (1, -1):
            start(ag_copy((first, 0, o, s, 1), 0))

    def ag_begin():
        for first in range(2):
            for s in (1, -1):
                start(ag_copy((first, s, 1, None, 0), 0))
        for first in range(2):
            ag_second(first, 0)

    def ag_arrive(m):
        key = m[1:]
        ag_copy(key, 1).wait_recv()
        first, s1, o, s2, i = key
        n1, n2 = SIZES[first], SIZES[1 - first]
        if s2 is None:
            if o < n1 // 2:
                start(ag_copy((first, s1, o + 1, None, 0), 0))
                ag_second(first, -s1 * o)
            elif s1 < 0:
                ag_second(first, o)
        elif i < n2 // 2:
            start(ag_copy((first, 0, o, s2, i + 1), 0))

    def ag_tick(t):
        for m in sorted((m for m in MSGS if m[0] == t), key=lambda m: (m[4] is not None, m[5])):
            ag_arrive(m)

    def pz_copy(s, t, back):
        half = t == NZ // 2
        rows = pl.ds(0 if s > 0 else 16, 16) if half else pl.ds(0, 32)
        ref = PF.at[:, wrap(z - s * (t - 1 + back), NZ), core, rows]
        n = (t - 1) * 2 + (s > 0)
        return remote(ref, ref, pz_s.at[n], pz_r.at[n], at(dz=s))

    def pz_tick(t):
        for s in (1, -1):
            if t > 0:
                pz_copy(s, t, 1).wait_recv()
            if t < NZ // 2:
                start(pz_copy(s, t + 1, 0))

    def pz_pair(side):
        ref = PF.at[:, :, side]
        return remote(ref, ref, pz_s.at[8], pz_r.at[8], sibling)

    def prepare():
        Ah[...], Al[...] = split(a_ref[...])
        for i in range(2):
            b = b_ref[i]
            Bh[i], Bl[i] = split(b)
            BTh[i], BTl[i] = split(b.T)

    def product(k):
        for h in range(2):
            out = None
            for F, base in ((FA, 0), (FB, 384)):
                left = split(F[k, 2 * h:2 * h + 2].reshape(256, 384))
                term = dot3(left, (Ah[base:base + 384], Al[base:base + 384]))
                out = term if out is None else out + term
            if k > 0:
                rows = slice(h * 256, h * 256 + 256)
                before = split(Yp[k - 1].reshape(512, 384))
                out = out - dot3((BTh[k - 1, rows], BTl[k - 1, rows]), before)
            Yp[k, 4 * h:4 * h + 4] = out.reshape(4, 2, 32, 384)

    def ex_copy(k):
        return remote(Yp.at[k, :, other], E.at[k], ex_s.at[k], ex_r.at[k], sibling)

    def ex_finish(k):
        ex_copy(k).wait_recv()
        E[k] = E[k] + Yp[k, :, core]

    def rs_rows(s, t):
        return (pl.ds(0, 16) if s > 0 else pl.ds(16, 16)) if t == 1 else pl.ds(0, 32)

    def rs_copy(k, s, t):
        n = (k * 4 + t - 1) * 2 + (s > 0)
        rows = rs_rows(s, t)
        return remote(E.at[k, wrap(z + s * (5 - t), NZ), rows], RB.at[k, int(s > 0), t - 1, rows],
                      rs_s.at[n], rs_r.at[n], at(dz=s))

    def rs_tick(k, t):
        for s in (1, -1):
            if t > 0:
                rs_copy(k, s, t).wait_recv()
                rows = rs_rows(s, t)
                block = wrap(z + s * (4 - t), NZ)
                E[k, block, rows] = E[k, block, rows] + RB[k, int(s > 0), t - 1, rows]
            if t < 4:
                start(rs_copy(k, s, t + 1))

    def columns_out(k):
        image = E[k, z]
        Yr[k] = image
        for j in range(3):
            flag = flag_ref[k, col * 3 + j].astype(F32)
            lanes = slice(j * BLK, (j + 1) * BLK)
            x_out[k, :, lanes] = -(image[:, lanes] * flag)

    root_z = lax.div(col, 4)
    root_core = lax.rem(lax.div(col, 2), 2)
    in_root_plane = z == root_z
    is_root = jnp.logical_and(in_root_plane, core == root_core)
    is_twin = jnp.logical_and(in_root_plane, core != root_core)
    even = lax.rem(col, 2) == 0
    from_root = wrap(z - root_z, NZ)
    half_rows = pl.ds(pl.multiple_of(core * 8, 8), 8)

    def spread(group, act):
        for F, mine in ((FA, even), (FB, jnp.logical_not(even))):
            @pl.when(jnp.logical_and(is_root, mine))
            def _():
                for n, d, xi, yi in group:
                    act(remote(F.at[:, xi, yi], Hc.at[:, xi, yi], rt_s.at[n], rt_r.at[n], sibling), None)
                    act(remote(F.at[:, xi, yi, half_rows], Hc.at[:, xi, yi, half_rows],
                               bc_s.at[n], bc_r.at[n], at(dz=d)), None)

        @pl.when(is_twin)
        def _():
            for n, d, xi, yi in group:
                whole = Hc.at[:, xi, yi]
                part = Hc.at[:, xi, yi, half_rows]
                act(remote(part, part, bc_s.at[n], bc_r.at[n], at(dz=d)),
                    remote(whole, whole, rt_s.at[n], rt_r.at[n], sibling))

    def hand_on(group, h, act):
        for way in (1, -1):
            @pl.when(from_root == (h if way > 0 else NZ - h))
            def _():
                for n, d, xi, yi in group:
                    if d == way:
                        part = Hc.at[:, xi, yi, half_rows]
                        c = remote(part, part, bc_s.at[n], bc_r.at[n], at(dz=d))
                        act(c if h < NZ - 1 else None, c)

    def bc_go(c, before):
        if before is not None:
            before.wait_recv()
        if c is not None:
            c.start()

    def bc_end(c, before):
        if c is not None:
            c.wait_send()

    def bc_group(t):
        return [(n, (1, -1)[(dx + dy) // 2 % 2] if (dx + dy) % 2 == 0 else (1, -1)[(dx - dy + 1) // 2 % 2], wrap(x + dx + NX, NX), wrap(y + dy + NY, NY))
                for n, (dx, dy) in enumerate(OFFSETS) if abs(dx) + abs(dy) == t]

    def bc_step(g, act=bc_go):
        for h in range(NZ - 1, -1, -1):
            if 0 <= g - h <= 6:
                group = bc_group(g - h)
                spread(group, act) if h == 0 else hand_on(group, h, act)

    def bc_local(act):
        for F, mine in ((FA, even), (FB, jnp.logical_not(even))):
            @pl.when(jnp.logical_and(is_root, mine))
            def _():
                cp = pltpu.make_async_copy(F, Hc, cp_s.at[0])
                cp.start() if act == "start" else cp.wait()

    def bc_pair(side):
        ref = Hc.at[:, :, :, pl.ds(pl.multiple_of(side * 8, 8), 8)]
        return remote(ref, ref, sx_s.at[0], sx_r.at[0], sibling)

    def bc_swap():
        @pl.when(jnp.logical_not(in_root_plane))
        def _():
            bc_pair(core).start()

    def bc_swapped():
        @pl.when(jnp.logical_not(in_root_plane))
        def _():
            bc_pair(other).wait_recv()
            bc_pair(core).wait_send()
        bc_local("wait")

    def reduced_factor(k):
        h = Hc[k].reshape(512, 384)
        if k > 0:
            h = h - dot3((BTh[k - 1], BTl[k - 1]), (Hh[k - 1], Hl[k - 1]))
        Hh[k], Hl[k] = split(h)

    def gram(k):
        if k == 0:
            TP[0:32] = dot3(split(Yr[0]), (Hh[0], Hl[0]), NT)
        else:
            left = Yr[k - 1:k + 1].reshape(64, 384)
            base = 32 if k == 1 else 128
            TP[base:base + 64] = dot3(split(left), (Hh[k], Hl[k]), NT)

    COLS = NX * NY
    BATCH = ((0, 16), (128, 8))

    def piece_of(b, at_col):
        base, n = BATCH[b]
        return TP.at[pl.ds(pl.multiple_of(base + lax.div(at_col, 4) * n, 8), n),
                     pl.ds(pl.multiple_of(lax.rem(at_col, 4) * BLK, BLK), BLK)]

    def at_col(o):
        return (row, wrap(col + o, COLS))

    def slots_of(buf, b):
        return buf.at[b, pl.ds(1, COLS - 1), pl.ds(0, BATCH[b][1])]

    def t_wait(buf, s_sem, r_sem, b, what):
        c = remote(slots_of(buf, b), slots_of(buf, b), s_sem.at[b], r_sem.at[b], at_col(1))
        getattr(c, what)()

    def t_first(b):
        for o in range(1, COLS):
            remote(piece_of(b, wrap(col + o, COLS)), R1.at[b, o, pl.ds(0, BATCH[b][1])],
                   t1_s.at[b], t1_r.at[b], at_col(o)).start()

    def t_second(b):
        rows = pl.ds(0, BATCH[b][1])
        own = piece_of(b, col)[...]
        t_wait(R1, t1_s, t1_r, b, "wait_recv")
        parts = [own] + [R1[b, o, rows] for o in range(1, COLS)]
        while len(parts) > 1:
            parts = [p + q for p, q in zip(parts[::2], parts[1::2])]
        R3[b, rows] = parts[0]
        for o in range(1, COLS):
            remote(R3.at[b, rows], R2.at[b, o, rows], t2_s.at[b], t2_r.at[b], at_col(o)).start()
        R2[b, 0, rows] = parts[0]

    def t_last(b):
        base, n = BATCH[b]
        t_wait(R2, t2_s, t2_r, b, "wait_recv")
        for i in range(COLS):
            TF[base + i // 4 * n:base + i // 4 * n + n, i % 4 * BLK:i % 4 * BLK + BLK] = R2[b, wrap(col - i + COLS, COLS), 0:n]

    def t_end(b):
        t_wait(R1, t1_s, t1_r, b, "wait_send")
        t_wait(R2, t2_s, t2_r, b, "wait_send")

    def drain():
        for c in sends:
            c.wait_send()
        sends.clear()

    def pivot_terms():
        b0, b1 = (Bh[0], Bl[0]), (Bh[1], Bl[1])
        mine = pl.ds(pl.multiple_of(row * 32, 32), 32)
        bt0, bt1 = (BTh[0, mine], BTl[0, mine]), (BTh[1, mine], BTl[1, mine])
        p0, p1 = split(PF[0].reshape(512, 512)), split(PF[1].reshape(512, 512))
        own0, own1, own2 = p_ref[0], p_ref[1], p_ref[2]
        q1 = own1 + dot3(split(dot3(bt0, p0, NT)), b0)
        U[0] = dot3(split(own0), b0)
        U[1] = dot3(split(q1), b1)
        inner = dot3(split(dot3(split(dot3(bt1, b0, NT)), p0)), b0) + dot3(bt1, p1, NT)
        Q[0] = q1
        Q[1] = own2 + dot3(split(inner), b1)

    ag_begin()
    pz_tick(0)
    bc_step(0)
    prepare()
    for g in range(1, 7):
        ag_tick(g)
        if g <= 4:
            pz_tick(g)
        if g == 5:
            start(pz_pair(core))
        bc_step(g)
    bc_local("start")
    product(0)
    start(ex_copy(0))
    bc_step(7)
    product(1)
    start(ex_copy(1))
    ex_finish(0)
    rs_tick(0, 0)
    bc_step(8)
    product(2)
    start(ex_copy(2))
    rs_tick(0, 1)
    ex_finish(1)
    rs_tick(1, 0)
    bc_step(9)
    rs_tick(0, 2)
    rs_tick(1, 1)
    ex_finish(2)
    rs_tick(2, 0)
    bc_step(10)
    rs_tick(0, 3)
    rs_tick(1, 2)
    rs_tick(2, 1)
    bc_step(11)
    rs_tick(0, 4)
    rs_tick(1, 3)
    rs_tick(2, 2)
    bc_step(12)
    bc_step(13)
    bc_swap()
    columns_out(0)
    pz_pair(other).wait_recv()
    pivot_terms()
    rs_tick(1, 4)
    rs_tick(2, 3)
    bc_swapped()
    reduced_factor(0)
    gram(0)
    reduced_factor(1)
    columns_out(1)
    gram(1)
    t_first(0)
    reduced_factor(2)
    rs_tick(2, 4)
    columns_out(2)
    gram(2)
    t_first(1)
    t_second(0)
    drain()
    for g in range(14):
        bc_step(g, bc_end)
    t_second(1)
    t_last(0)
    d_out[0] = p_ref[0] + TF[0:32]
    par_out[0] = TF[32:64] - U[0]
    d_out[1] = Q[0] + TF[64:96]
    t_last(1)
    par_out[1] = TF[128:160] - U[1]
    d_out[2] = Q[1] + TF[160:192]
    t_end(0)
    t_end(1)


def deliver(*refs):
    for src, dst in zip(refs[:3], refs[3:]):
        dst[...] = src[...]


def body(front, structure, factor_front, factor_border, pivot_inverse):
    vmem = pl.BlockSpec(memory_space=pltpu.VMEM)
    dma = lambda n: pltpu.SemaphoreType.DMA((n,))
    v = lambda *shape: pltpu.VMEM(shape, F32)
    h = lambda *shape: pltpu.VMEM(shape, jnp.bfloat16)
    n_ag = len(MSGS)
    shapes = (
        jax.ShapeDtypeStruct((3, 32, 384), F32),
        jax.ShapeDtypeStruct((2, 32, 512), F32),
        jax.ShapeDtypeStruct((3, 32, 512), F32),
    )
    results = pl.pallas_call(
        kernel,
        out_shape=shapes,
        in_specs=[pl.BlockSpec(memory_space=pltpu.SMEM)] + [vmem] * 4,
        out_specs=(vmem,) * 3,
        scratch_shapes=[
            v(3, NX, NY, 16, 384), v(3, NX, NY, 16, 384),
            v(2, NZ, 2, 32, 512),
            v(3, NZ, 2, 32, 384),
            v(3, NZ, 32, 384),
            v(3, 2, 4, 32, 384),
            v(3, NX, NY, 16, 384),
            h(768, 384), h(768, 384),
            h(2, 512, 512), h(2, 512, 512), h(2, 512, 512), h(2, 512, 512),
            h(3, 512, 384), h(3, 512, 384),
            v(3, 32, 384),
            v(192, 512),
            v(2, 32, 16, 128), v(2, 32, 16, 128), v(2, 16, 128),
            v(192, 512),
            v(2, 32, 512), v(2, 32, 512),
            dma(n_ag), dma(n_ag),
            dma(9), dma(9),
            dma(3), dma(3),
            dma(24), dma(24),
            dma(32), dma(32),
            dma(32), dma(32),
            dma(1), dma(1),
            dma(1),
            dma(2), dma(2), dma(2), dma(2),
        ],
        compiler_params=pltpu.CompilerParams(
            collective_id=0, has_side_effects=True, vmem_limit_bytes=56 * 2**20),
        cost_estimate=pl.CostEstimate(flops=8 * 10**9, bytes_accessed=5 * 10**6, transcendentals=0),
    )(structure, front, jnp.transpose(factor_front, (0, 2, 1)), factor_border, pivot_inverse)
    return pl.pallas_call(deliver, out_shape=shapes, in_specs=[vmem] * 3, out_specs=(vmem,) * 3)(*results)


def solution(mesh):
    return jax.shard_map(
        body,
        mesh=mesh,
        in_specs=(P("row", "col"), P(), P(None, "row", "col"), P(), P(None, "row", None)),
        out_specs=(P(None, "row", "col"), P(None, "row", None), P(None, "row", None)),
        check_vma=False,
    )
```

time: 152 us -> 113 us (0.74)
  the two profiles are of different devices: /device:TPU:2 before, /device:TPU:8 now
where the time goes in v2:
time: 113 us
  Pallas kernels  112 us (99%)
    pallas_call x1, Pallas kernels, body(): pl.pallas_call(kernel, out_shape=shapes, in_specs=[pl.BlockSpec(memory_sp...  111 us

profile of v2, /device:TPU:8, one launch (start us, length us, event | category | flops | bytes accessed | tf_op | source)
XLA Modules:
  0.0 113.1 jit_solution(17944653736815210158)
XLA Ops:
  0.6 110.6 %shard_map.76 = (f32[3,32,384]{2,1,0:T(8,128)}, f32[2,32,512]{2,1,0:T(8,128)}, f32[3,32,512]{2,1,0:T(8,128)}) custom-call(s32[3,96]{1,0:T(4,128)} %flag_ref.1, f32[768,384]{1,0:T(8,128)} %a_ref.1, f32[3,16,768]{2,1,0:T(8,128)} %bitcast.1, f32[2,512,512]{2,1,0:T(8,128)} %b_ref.1, f32[3,32,512]{2,1,0:T(8,128)} %p_ref.1), custom_call_target="tpu_custom_call" | custom-call | flops 8000000000 | bytes 5000000 | tf_op jit(solution)/shard_map/pallas_call | solution.py:466
  111.3 1.8 %shard_map.77 = (f32[3,32,384]{2,1,0:T(8,128)}, f32[2,32,512]{2,1,0:T(8,128)}, f32[3,32,512]{2,1,0:T(8,128)}) custom-call(f32[3,32,384]{2,1,0:T(8,128)} %get-tuple-element.6.refs_0_, f32[2,32,512]{2,1,0:T(8,128)} %get-tuple-element.7.refs_1_, f32[3,32,512]{2,1,0:T(8,128)} %get-tuple-element.8.refs_2_), custom_call_target="tpu_custom_call" | custom-call | tf_op jit(solution)/shard_map/pallas_call | solution.py:500

commit v3 on v2

--- a/solution.py
+++ b/solution.py
@@ -224,34 +224,43 @@
     is_twin = jnp.logical_and(in_root_plane, core != root_core)
     even = lax.rem(col, 2) == 0
     from_root = wrap(z - root_z, NZ)
+    hop = jnp.minimum(from_root, NZ - from_root)
+    onward = jnp.where(from_root < NZ // 2, 1, -1)
     half_rows = pl.ds(pl.multiple_of(core * 8, 8), 8)
 
     def spread(group, act):
         for F, mine in ((FA, even), (FB, jnp.logical_not(even))):
             @pl.when(jnp.logical_and(is_root, mine))
             def _():
-                for n, d, xi, yi in group:
+                for n, xi, yi in group:
                     act(remote(F.at[:, xi, yi], Hc.at[:, xi, yi], rt_s.at[n], rt_r.at[n], sibling), None)
-                    act(remote(F.at[:, xi, yi, half_rows], Hc.at[:, xi, yi, half_rows],
-                               bc_s.at[n], bc_r.at[n], at(dz=d)), None)
+                for n, xi, yi in group:
+                    for d in (1, -1):
+                        act(remote(F.at[:, xi, yi, half_rows], Hc.at[:, xi, yi, half_rows],
+                                   bc_s.at[n * 2 + (d > 0)], bc_r.at[n], at(dz=d)), None)
 
         @pl.when(is_twin)
         def _():
-            for n, d, xi, yi in group:
+            for n, xi, yi in group:
                 whole = Hc.at[:, xi, yi]
                 part = Hc.at[:, xi, yi, half_rows]
-                act(remote(part, part, bc_s.at[n], bc_r.at[n], at(dz=d)),
-                    remote(whole, whole, rt_s.at[n], rt_r.at[n], sibling))
+                for d in (1, -1):
+                    act(remote(part, part, bc_s.at[n * 2 + (d > 0)], bc_r.at[n], at(dz=d)),
+                        remote(whole, whole, rt_s.at[n], rt_r.at[n], sibling) if d > 0 else None)
 
     def hand_on(group, h, act):
-        for way in (1, -1):
-            @pl.when(from_root == (h if way > 0 else NZ - h))
-            def _():
-                for n, d, xi, yi in group:
-                    if d == way:
-                        part = Hc.at[:, xi, yi, half_rows]
-                        c = remote(part, part, bc_s.at[n], bc_r.at[n], at(dz=d))
-                        act(c if h < NZ - 1 else None, c)
+        def run(forward):
+            for n, xi, yi in group:
+                part = Hc.at[:, xi, yi, half_rows]
+                c = remote(part, part, bc_s.at[n * 2], bc_r.at[n], at(dz=onward))
+                act(c if forward else None, c)
+        if h < 3:
+            pl.when(hop == h)(lambda: run(True))
+        elif h == 3:
+            pl.when(from_root == 3)(lambda: run(True))
+            pl.when(from_root == NZ - 3)(lambda: run(False))
+        else:
+            pl.when(hop == h)(lambda: run(False))
 
     def bc_go(c, before):
         if before is not None:
@@ -264,11 +273,11 @@
             c.wait_send()
 
     def bc_group(t):
-        return [(n, (1, -1)[(dx + dy) // 2 % 2] if (dx + dy) % 2 == 0 else (1, -1)[(dx - dy + 1) // 2 % 2], wrap(x + dx + NX, NX), wrap(y + dy + NY, NY))
+        return [(n, wrap(x + dx + NX, NX), wrap(y + dy + NY, NY))
                 for n, (dx, dy) in enumerate(OFFSETS) if abs(dx) + abs(dy) == t]
 
     def bc_step(g, act=bc_go):
-        for h in range(NZ - 1, -1, -1):
+        for h in range(NZ // 2, -1, -1):
             if 0 <= g - h <= 6:
                 group = bc_group(g - h)
                 spread(group, act) if h == 0 else hand_on(group, h, act)
@@ -404,19 +413,14 @@
     ex_finish(2)
     rs_tick(2, 0)
     bc_step(10)
+    bc_swap()
     rs_tick(0, 3)
     rs_tick(1, 2)
     rs_tick(2, 1)
-    bc_step(11)
     rs_tick(0, 4)
     rs_tick(1, 3)
     rs_tick(2, 2)
-    bc_step(12)
-    bc_step(13)
-    bc_swap()
     columns_out(0)
-    pz_pair(other).wait_recv()
-    pivot_terms()
     rs_tick(1, 4)
     rs_tick(2, 3)
     bc_swapped()
@@ -432,10 +436,12 @@
     gram(2)
     t_first(1)
     t_second(0)
+    t_second(1)
+    pz_pair(other).wait_recv()
+    pivot_terms()
     drain()
-    for g in range(14):
+    for g in range(11):
         bc_step(g, bc_end)
-    t_second(1)
     t_last(0)
     d_out[0] = p_ref[0] + TF[0:32]
     par_out[0] = TF[32:64] - U[0]
@@ -487,7 +493,7 @@
             dma(9), dma(9),
             dma(3), dma(3),
             dma(24), dma(24),
-            dma(32), dma(32),
+            dma(64), dma(32),
             dma(32), dma(32),
             dma(1), dma(1),
             dma(1),

time: 113 us -> 112 us (level)
    pallas_call x1, Pallas kernels: 111 us -> 109 us  [body(): pl.pallas_call(kernel, out_shape=shapes, in_specs=[pl.BlockSpec(memory_sp...]
where the time goes in v3:
time: 112 us
  Pallas kernels  111 us (99%)
    pallas_call x1, Pallas kernels, body(): pl.pallas_call(kernel, out_shape=shapes, in_specs=[pl.BlockSpec(memory_sp...  109 us

profile of v3, /device:TPU:8, one launch (start us, length us, event | category | flops | bytes accessed | tf_op | source)
XLA Modules:
  0.0 111.5 jit_solution(3659908727124315618)
XLA Ops:
  0.6 109.0 %shard_map.76 = (f32[3,32,384]{2,1,0:T(8,128)}, f32[2,32,512]{2,1,0:T(8,128)}, f32[3,32,512]{2,1,0:T(8,128)}) custom-call(s32[3,96]{1,0:T(4,128)} %flag_ref.1, f32[768,384]{1,0:T(8,128)} %a_ref.1, f32[3,16,768]{2,1,0:T(8,128)} %bitcast.1, f32[2,512,512]{2,1,0:T(8,128)} %b_ref.1, f32[3,32,512]{2,1,0:T(8,128)} %p_ref.1), custom_call_target="tpu_custom_call" | custom-call | flops 8000000000 | bytes 5000000 | tf_op jit(solution)/shard_map/pallas_call | solution.py:472
  109.7 1.8 %shard_map.77 = (f32[3,32,384]{2,1,0:T(8,128)}, f32[2,32,512]{2,1,0:T(8,128)}, f32[3,32,512]{2,1,0:T(8,128)}) custom-call(f32[3,32,384]{2,1,0:T(8,128)} %get-tuple-element.6.refs_0_, f32[2,32,512]{2,1,0:T(8,128)} %get-tuple-element.7.refs_1_, f32[3,32,512]{2,1,0:T(8,128)} %get-tuple-element.8.refs_2_), custom_call_target="tpu_custom_call" | custom-call | tf_op jit(solution)/shard_map/pallas_call | solution.py:506
